TPU v7x, 32 devices: a whole 2x2x4 slice. The times are simulated.
32 devices in a mesh: seq: 8 (over y, x, core), mp: 4 (over z).
Axes of the slice: x: 2, y: 2, z: 4, core: 2. Of those that a mesh axis runs over, the one named last changes fastest.
Arguments:
- projected: bfloat16 [3, 8192, 1024], P(None, 'mp', 'seq'), may hold values from -6 to 6
- short_taps: float32 [3, 3, 8192], replicated, may hold values from -4 to 4
- skip_gain: float32 [8192], replicated, may hold values from -4 to 4
- residue: float32 [2048, 16], P('seq'), may hold values from -4 to 4
- decay_rate: float32 [2048, 16], P('seq'), may hold values from 0.00048828125 to 0.05
Outputs:
- gated: bfloat16 [8192, 1024], P('mp', 'seq')
All inputs are finite; a program needn't handle non-finite values.
Results may differ from a plain program's by a relative error of at most 0.012.
Values may be sent and summed in bfloat16 or wider, within the bound.
A program may use at most 128 MiB of HBM per device.

v0:
```python
import functools

import jax
import jax.numpy as jnp
from jax import lax
from jax.experimental import pallas as pl
from jax.experimental.pallas import tpu as pltpu
from jax.sharding import PartitionSpec as P

MESH = pl.DeviceIdType.MESH
LANES = 128
ROWS = 8


def rows_of(first, count=ROWS):
    return pl.ds(pl.multiple_of(first, ROWS), count)


def kernel(
    seq_count,
    modes,
    half_count,
    length,
    filters,
    projected,
    taps_hbm,
    skip_hbm,
    residue,
    rate,
    out,
    streams,
    taps_raw,
    skip,
    taps,
    laid,
    product,
    mixed_q,
    local,
    own_params,
    params,
    rates,
    weights,
    decay,
    block_decay,
    halo_out,
    halo_in,
    own_state,
    states,
    carry,
    in_sem,
    tap_sem,
    param_send,
    param_recv,
    halo_send,
    halo_recv,
    state_send,
    state_recv,
):
    me = lax.axis_index("seq")
    group = lax.axis_index("mp")
    block_count = half_count * ROWS
    width = block_count * LANES
    half_rows = length * ROWS

    in_copies = [
        pltpu.make_async_copy(projected.at[s], streams.at[s], in_sem.at[s]) for s in range(3)
    ]
    tap_copy = pltpu.make_async_copy(
        taps_hbm.at[:, :, pl.ds(pl.multiple_of(group * width, LANES), width)],
        taps_raw,
        tap_sem.at[0],
    )
    skip_copy = pltpu.make_async_copy(
        skip_hbm.at[rows_of(group * block_count, block_count)], skip, tap_sem.at[1]
    )
    for copy in in_copies:
        copy.start()
    tap_copy.start()
    skip_copy.start()

    barrier = pltpu.get_barrier_semaphore()

    def greet(step, _):
        peer = lax.rem(me + step, seq_count)
        pl.semaphore_signal(barrier, inc=1, device_id={"seq": peer}, device_id_type=MESH)
        return 0

    lax.fori_loop(1, seq_count, greet, 0)
    own_params[0] = rate[...]
    own_params[1] = residue[...] * jnp.sqrt(rate[...])
    params[me] = own_params[...]
    pl.semaphore_wait(barrier, seq_count - 1)

    def param_copy(step):
        peer = lax.rem(me + step, seq_count)
        return pltpu.make_async_remote_copy(
            src_ref=own_params,
            dst_ref=params.at[me],
            send_sem=param_send.at[step],
            recv_sem=param_recv.at[step],
            device_id={"seq": peer},
            device_id_type=MESH,
        )

    def send_params(step, _):
        param_copy(step).start()
        return 0

    lax.fori_loop(1, seq_count, send_params, 0)

    eye = (
        lax.broadcasted_iota(jnp.int32, (LANES, LANES), 0)
        == lax.broadcasted_iota(jnp.int32, (LANES, LANES), 1)
    ).astype(jnp.bfloat16)
    across = (((1,), (1,)), ((), ()))
    for s in range(3):
        in_copies[s].wait()
        for pair in range(block_count // 2):
            turned = lax.dot_general(
                eye,
                streams[s, pair * 256 : pair * 256 + 256, :],
                across,
                preferred_element_type=jnp.float32,
            )
            for side in range(2):
                half, row = divmod(pair * 2 + side, ROWS)
                laid[pl.ds((s * half_count + half) * half_rows + row, length, stride=ROWS), :] = (
                    turned[:, side * LANES : (side + 1) * LANES]
                )

    def laid_row(s, half, t):
        return laid[rows_of((s * half_count + half) * half_rows + t * ROWS), :]

    for s in range(3):
        for back in range(2):
            pieces = [laid_row(s, half, length - 2 + back) for half in range(half_count)]
            halo_out[s * 2 + back] = jnp.concatenate(pieces, axis=0).astype(jnp.bfloat16)

    halo_copy = pltpu.make_async_remote_copy(
        src_ref=halo_out,
        dst_ref=halo_in,
        send_sem=halo_send,
        recv_sem=halo_recv,
        device_id={"seq": lax.rem(me + 1, seq_count)},
        device_id_type=MESH,
    )

    @pl.when(me < seq_count - 1)
    def _():
        halo_copy.start()

    tap_copy.wait()
    skip_copy.wait()
    for lag in range(3):
        for s in range(3):
            for block in range(block_count):
                taps[lag * 3 + s, block : block + 1, :] = taps_raw[
                    lag, s : s + 1, block * LANES : (block + 1) * LANES
                ]

    def tap_rows(half):
        return [
            [taps[lag * 3 + s, half * ROWS : (half + 1) * ROWS, :] for lag in range(3)]
            for s in range(3)
        ]

    def put_mixed(half, t, now, before, earlier, tap):
        q, k, v = [
            tap[s][0] * now[s] + tap[s][1] * before[s] + tap[s][2] * earlier[s] for s in range(3)
        ]
        at = rows_of(half * half_rows + t * ROWS)
        mixed_q[at, :] = q
        product[at, :] = (k * v).astype(jnp.bfloat16).astype(jnp.float32)

    for half in range(half_count):
        tap = tap_rows(half)

        def mix(t, past, half=half, tap=tap):
            before, earlier = past
            now = [laid_row(s, half, t) for s in range(3)]
            put_mixed(half, t, now, before, earlier, tap)
            return now, before

        first = [[laid_row(s, half, t) for s in range(3)] for t in range(2)]
        lax.fori_loop(2, length, mix, (first[1], first[0]), unroll=6)

    @pl.when(me > 0)
    def _():
        halo_copy.wait_recv()

    @pl.when(me == 0)
    def _():
        halo_in[...] = jnp.zeros(halo_in.shape, halo_in.dtype)

    for half in range(half_count):
        tap = tap_rows(half)
        past = [
            [
                halo_in[s * 2 + back].astype(jnp.float32)[half * ROWS : (half + 1) * ROWS]
                for s in range(3)
            ]
            for back in range(2)
        ]
        first = [[laid_row(s, half, t) for s in range(3)] for t in range(2)]
        put_mixed(half, 0, first[0], past[1], past[0], tap)
        put_mixed(half, 1, first[1], first[0], past[1], tap)

    def take_params(step, _):
        param_copy(step).wait_recv()
        return 0

    lax.fori_loop(1, seq_count, take_params, 0)
    for block in range(block_count):
        half, row = divmod(block, ROWS)
        for kind, target in ((0, rates), (1, weights)):
            if filters >= LANES:
                per = filters // LANES
                lane = (block % per) * LANES
                piece = params[block // per, kind, :, lane : lane + LANES]
            else:
                per = LANES // filters
                piece = jnp.concatenate(
                    [params[block * per + part, kind] for part in range(per)], axis=1
                )
            target[pl.ds(half * modes * ROWS + row, modes, stride=ROWS), :] = piece
    decay[...] = jnp.exp(-rates[...])
    block_decay[...] = jnp.exp(-float(length) * rates[...])

    def of_modes(ref, half):
        first = half * modes * ROWS
        return [ref[first + n * ROWS : first + (n + 1) * ROWS, :] for n in range(modes)]

    def state_copy(half, step):
        peer = lax.rem(me + step, seq_count)
        return pltpu.make_async_remote_copy(
            src_ref=own_state.at[half],
            dst_ref=states.at[me, half],
            send_sem=state_send.at[half, step],
            recv_sem=state_recv.at[half, step],
            device_id={"seq": peer},
            device_id_type=MESH,
        )

    for half in range(half_count):
        rate_of = of_modes(decay, half)

        def gather_state(t, held, half=half, rate_of=rate_of):
            value = product[rows_of(half * half_rows + t * ROWS), :]
            return [rate_of[n] * held[n] + value for n in range(modes)]

        held = lax.fori_loop(
            0,
            length,
            gather_state,
            [jnp.zeros((ROWS, LANES), jnp.float32)] * modes,
            unroll=8,
        )
        own_state[half] = jnp.concatenate(held, axis=0).astype(jnp.bfloat16)

        def send_state(step, _, half=half):
            state_copy(half, step).start()
            return 0

        lax.fori_loop(1, seq_count - me, send_state, 0)

    for half in range(half_count):
        rate_of = of_modes(decay, half)
        weight_of = of_modes(weights, half)

        def convolve(t, held, half=half, rate_of=rate_of, weight_of=weight_of):
            at = rows_of(half * half_rows + t * ROWS)
            value = product[at, :]
            held = [rate_of[n] * held[n] + value for n in range(modes)]
            local[at, :] = tree_sum([weight_of[n] * held[n] for n in range(modes)])
            return held

        lax.fori_loop(
            0, length, convolve, [jnp.zeros((ROWS, LANES), jnp.float32)] * modes, unroll=4
        )

    for half in range(half_count):
        mode_rows = modes * ROWS
        first = half * mode_rows
        carry[...] = jnp.zeros(carry.shape, jnp.float32)

        def take_state(sender, _, half=half, first=first):
            state_copy(half, me - sender).wait_recv()
            carry[...] = carry[...] * block_decay[first : first + mode_rows, :] + states[
                sender, half
            ].astype(jnp.float32)
            return 0

        lax.fori_loop(0, me, take_state, 0)
        carry[...] = carry[...] * weights[first : first + mode_rows, :]
        rate_of = of_modes(decay, half)
        skip_here = skip[half * ROWS : (half + 1) * ROWS, :]

        def finish(t, held, half=half, rate_of=rate_of, skip_here=skip_here):
            at = rows_of(half * half_rows + t * ROWS)
            held = [rate_of[n] * held[n] for n in range(modes)]
            long_part = (local[at, :] + tree_sum(held)).astype(jnp.bfloat16).astype(jnp.float32)
            local[at, :] = mixed_q[at, :] * (long_part + skip_here * product[at, :])
            return held

        lax.fori_loop(0, length, finish, of_modes(carry, 0), unroll=4)
        for row in range(ROWS):
            gated = local[pl.ds(half * half_rows + row, length, stride=ROWS), :].astype(jnp.bfloat16)
            first_channel = (half * ROWS + row) * LANES
            out[first_channel : first_channel + LANES, :] = lax.dot_general(
                eye, gated, across, preferred_element_type=jnp.float32
            ).astype(jnp.bfloat16)

    def drain_params(step, _):
        param_copy(step).wait_send()
        return 0

    lax.fori_loop(1, seq_count, drain_params, 0)

    @pl.when(me < seq_count - 1)
    def _():
        halo_copy.wait_send()

    def drain_states(step, _):
        for half in range(half_count):
            state_copy(half, step).wait_send()
        return 0

    lax.fori_loop(1, seq_count - me, drain_states, 0)


def tree_sum(terms):
    while len(terms) > 1:
        terms = [terms[i] + terms[i + 1] for i in range(0, len(terms), 2)]
    return terms[0]


def body(projected, short_taps, skip_gain, residue, decay_rate):
    seq_count = lax.axis_size("seq")
    _, width, length = projected.shape
    filters, modes = residue.shape
    block_count = width // LANES
    half_count = block_count // ROWS
    call = functools.partial(kernel, seq_count, modes, half_count, length, filters)
    vmem = pl.BlockSpec(memory_space=pltpu.VMEM)
    anywhere = pl.BlockSpec(memory_space=pl.ANY)
    mode_rows = modes * ROWS
    f32, bf16 = jnp.float32, jnp.bfloat16
    dma = pltpu.SemaphoreType.DMA
    return pl.pallas_call(
        call,
        out_shape=jax.ShapeDtypeStruct((width, length), bf16),
        in_specs=[anywhere, anywhere, anywhere, vmem, vmem],
        out_specs=vmem,
        scratch_shapes=[
            pltpu.VMEM((3, width, length), bf16),
            pltpu.VMEM((3, 3, width), f32),
            pltpu.VMEM((block_count, LANES), f32),
            pltpu.VMEM((9, block_count, LANES), f32),
            pltpu.VMEM((3 * length * block_count, LANES), f32),
            pltpu.VMEM((length * block_count, LANES), f32),
            pltpu.VMEM((length * block_count, LANES), f32),
            pltpu.VMEM((length * block_count, LANES), f32),
            pltpu.VMEM((2, modes, filters), f32),
            pltpu.VMEM((seq_count, 2, modes, filters), f32),
            pltpu.VMEM((half_count * mode_rows, LANES), f32),
            pltpu.VMEM((half_count * mode_rows, LANES), f32),
            pltpu.VMEM((half_count * mode_rows, LANES), f32),
            pltpu.VMEM((half_count * mode_rows, LANES), f32),
            pltpu.VMEM((6, block_count, LANES), bf16),
            pltpu.VMEM((6, block_count, LANES), bf16),
            pltpu.VMEM((half_count, mode_rows, LANES), bf16),
            pltpu.VMEM((seq_count, half_count, mode_rows, LANES), bf16),
            pltpu.VMEM((mode_rows, LANES), f32),
            dma((3,)),
            dma((2,)),
            dma((seq_count,)),
            dma((seq_count,)),
            dma,
            dma,
            dma((half_count, seq_count)),
            dma((half_count, seq_count)),
        ],
        compiler_params=pltpu.CompilerParams(
            collective_id=0, has_side_effects=True, vmem_limit_bytes=40 * 1024 * 1024
        ),
    )(
        projected,
        short_taps,
        skip_gain.reshape(skip_gain.shape[0] // LANES, LANES),
        residue.T,
        decay_rate.T,
    )


def solution(mesh):
    in_specs = (P(None, "mp", "seq"), P(), P(), P("seq", None), P("seq", None))
    out_specs = P("mp", "seq")
    return jax.shard_map(body, mesh=mesh, in_specs=in_specs, out_specs=out_specs, check_vma=False)
```

profile of v0, /device:TPU:5, one launch (start us, length us, event | category | flops | bytes accessed | tf_op | source)
XLA Modules:
  0.0 22.4 jit_solution(7503584754990349473)
XLA Ops:
  0.0 0.0 copy-start
  0.0 1.4 %copy-done = bf16[3,2048,128]{2,1,0:T(8,128)(2,1)S(1)} copy-done((bf16[3,2048,128]{2,1,0:T(8,128)(2,1)S(1)}, bf16[3,2048,128]{2,1,0:T(8,128)(2,1)}, u32[]{:S(2)}) %copy-start) | copy-done | bytes 1572888
  1.4 0.0 copy-start.1
  1.4 1.0 %copy-done.1 = f32[3,3,8192]{2,1,0:T(4,128)S(1)} copy-done((f32[3,3,8192]{2,1,0:T(4,128)S(1)}, f32[3,3,8192]{2,1,0:T(4,128)}, u32[]{:S(2)}) %copy-start.1) | copy-done | bytes 294936
  2.4 0.0 copy-start.2
  2.4 0.8 %copy-done.2 = f32[8192]{0:T(1024)S(1)} copy-done((f32[8192]{0:T(1024)S(1)}, f32[8192]{0:T(1024)}, u32[]{:S(2)}) %copy-start.2) | copy-done | bytes 32792
  3.2 0.0 copy-start.3
  3.2 0.7 %copy-done.3 = f32[256,16]{0,1:T(8,128)S(1)} copy-done((f32[256,16]{0,1:T(8,128)S(1)}, f32[256,16]{0,1:T(8,128)}, u32[]{:S(2)}) %copy-start.3) | copy-done | bytes 16408
  3.9 0.0 copy-start.4
  3.9 0.7 %copy-done.4 = f32[256,16]{0,1:T(8,128)S(1)} copy-done((f32[256,16]{0,1:T(8,128)S(1)}, f32[256,16]{0,1:T(8,128)}, u32[]{:S(2)}) %copy-start.4) | copy-done | bytes 16408
  4.6 17.0 %shard_map.55 = bf16[2048,128]{1,0:T(8,128)(2,1)S(1)} custom-call(bf16[3,2048,128]{2,1,0:T(8,128)(2,1)S(1)} %copy-done, f32[3,3,8192]{2,1,0:T(4,128)S(1)} %copy-done.1, f32[64,128]{1,0:T(8,128)S(1)} %bitcast.3, f32[16,256]{1,0:T(8,128)S(1)} %bitcast.4, f32[16,256]{1,0:T(8,128)S(1)} %bitcast.5), custom_call_target="tpu_custom_call" | custom-call | tf_op jit(solution)/shard_map/pallas_call | solution.py:349
  21.6 0.8 %copy.7 = bf16[2048,128]{1,0:T(8,128)(2,1)} copy(bf16[2048,128]{1,0:T(8,128)(2,1)S(1)} %shard_map.55) | data formatting | bytes 1048576
Async XLA Ops:
  0.0 1.4 %copy-start = (bf16[3,2048,128]{2,1,0:T(8,128)(2,1)S(1)}, bf16[3,2048,128]{2,1,0:T(8,128)(2,1)}, u32[]{:S(2)}) copy-start(bf16[3,2048,128]{2,1,0:T(8,128)(2,1)} %projected.1) | copy-start | bytes 4718596
  1.4 1.0 %copy-start.1 = (f32[3,3,8192]{2,1,0:T(4,128)S(1)}, f32[3,3,8192]{2,1,0:T(4,128)}, u32[]{:S(2)}) copy-start(f32[3,3,8192]{2,1,0:T(4,128)} %taps_hbm.1) | copy-start | bytes 884740
  2.4 0.8 %copy-start.2 = (f32[8192]{0:T(1024)S(1)}, f32[8192]{0:T(1024)}, u32[]{:S(2)}) copy-start(f32[8192]{0:T(1024)} %param.7) | copy-start | bytes 98308
  3.2 0.7 %copy-start.3 = (f32[256,16]{0,1:T(8,128)S(1)}, f32[256,16]{0,1:T(8,128)}, u32[]{:S(2)}) copy-start(f32[256,16]{0,1:T(8,128)} %param.8) | copy-start | bytes 49156
  3.9 0.7 %copy-start.4 = (f32[256,16]{0,1:T(8,128)S(1)}, f32[256,16]{0,1:T(8,128)}, u32[]{:S(2)}) copy-start(f32[256,16]{0,1:T(8,128)} %param.9) | copy-start | bytes 49156
where the time goes:
time: 22.7 us; the launch traced here: 22.4 us
  Pallas kernels  17 us (75%)
  local copies, waits for them, and re-layouts  5.39 us (24%)
    pallas_call x1, Pallas kernels, body(): pl.pallas_call(call, out_shape=jax.ShapeDtypeStruct((width, length), bf16...  17 us
    unnamed x11, local copies, waits for them, and re-layouts  5.39 us

commit v1 on v0

--- a/solution.py
+++ b/solution.py
@@ -25,9 +25,11 @@
     projected,
     taps_hbm,
     skip_hbm,
+    residue_hbm,
+    rate_hbm,
+    out,
     residue,
     rate,
-    out,
     streams,
     taps_raw,
     skip,
@@ -42,17 +44,24 @@
     weights,
     decay,
     block_decay,
+    pair_decay,
     halo_out,
     halo_in,
     own_state,
+    mate_state,
+    pair_state,
     states,
     carry,
+    staged,
     in_sem,
+    out_sem,
     tap_sem,
     param_send,
     param_recv,
     halo_send,
     halo_recv,
+    mate_send,
+    mate_recv,
     state_send,
     state_recv,
 ):
@@ -61,6 +70,11 @@
     block_count = half_count * ROWS
     width = block_count * LANES
     half_rows = length * ROWS
+    mode_rows = modes * ROWS
+    side = lax.rem(me, 2)
+    pair = lax.div(me, 2)
+    pair_count = seq_count // 2
+    mate = me + 1 - 2 * side
 
     in_copies = [
         pltpu.make_async_copy(projected.at[s], streams.at[s], in_sem.at[s]) for s in range(3)
@@ -73,6 +87,10 @@
     skip_copy = pltpu.make_async_copy(
         skip_hbm.at[rows_of(group * block_count, block_count)], skip, tap_sem.at[1]
     )
+    rate_copy = pltpu.make_async_copy(rate_hbm, rate, tap_sem.at[2])
+    residue_copy = pltpu.make_async_copy(residue_hbm, residue, tap_sem.at[3])
+    rate_copy.start()
+    residue_copy.start()
     for copy in in_copies:
         copy.start()
     tap_copy.start()
@@ -86,27 +104,32 @@
         return 0
 
     lax.fori_loop(1, seq_count, greet, 0)
+    rate_copy.wait()
+    residue_copy.wait()
     own_params[0] = rate[...]
     own_params[1] = residue[...] * jnp.sqrt(rate[...])
     params[me] = own_params[...]
     pl.semaphore_wait(barrier, seq_count - 1)
 
-    def param_copy(step):
+    def param_copy(kind, step):
         peer = lax.rem(me + step, seq_count)
         return pltpu.make_async_remote_copy(
-            src_ref=own_params,
-            dst_ref=params.at[me],
-            send_sem=param_send.at[step],
-            recv_sem=param_recv.at[step],
+            src_ref=own_params.at[kind],
+            dst_ref=params.at[me, kind],
+            send_sem=param_send.at[kind, step],
+            recv_sem=param_recv.at[kind, step],
             device_id={"seq": peer},
             device_id_type=MESH,
         )
 
-    def send_params(step, _):
-        param_copy(step).start()
-        return 0
-
-    lax.fori_loop(1, seq_count, send_params, 0)
+    def send_params(kind):
+        def send(step, _):
+            param_copy(kind, step).start()
+            return 0
+
+        lax.fori_loop(1, seq_count, send, 0)
+
+    send_params(0)
 
     eye = (
         lax.broadcasted_iota(jnp.int32, (LANES, LANES), 0)
@@ -115,17 +138,17 @@
     across = (((1,), (1,)), ((), ()))
     for s in range(3):
         in_copies[s].wait()
-        for pair in range(block_count // 2):
+        for couple in range(block_count // 2):
             turned = lax.dot_general(
                 eye,
-                streams[s, pair * 256 : pair * 256 + 256, :],
+                streams[s, couple * 256 : couple * 256 + 256, :],
                 across,
                 preferred_element_type=jnp.float32,
             )
-            for side in range(2):
-                half, row = divmod(pair * 2 + side, ROWS)
+            for part in range(2):
+                half, row = divmod(couple * 2 + part, ROWS)
                 laid[pl.ds((s * half_count + half) * half_rows + row, length, stride=ROWS), :] = (
-                    turned[:, side * LANES : (side + 1) * LANES]
+                    turned[:, part * LANES : (part + 1) * LANES]
                 )
 
     def laid_row(s, half, t):
@@ -149,6 +172,7 @@
     def _():
         halo_copy.start()
 
+    send_params(1)
     tap_copy.wait()
     skip_copy.wait()
     for lag in range(3):
@@ -205,14 +229,14 @@
         put_mixed(half, 0, first[0], past[1], past[0], tap)
         put_mixed(half, 1, first[1], first[0], past[1], tap)
 
-    def take_params(step, _):
-        param_copy(step).wait_recv()
-        return 0
-
-    lax.fori_loop(1, seq_count, take_params, 0)
-    for block in range(block_count):
-        half, row = divmod(block, ROWS)
-        for kind, target in ((0, rates), (1, weights)):
+    def take_params(kind, target):
+        def take(step, _):
+            param_copy(kind, step).wait_recv()
+            return 0
+
+        lax.fori_loop(1, seq_count, take, 0)
+        for block in range(block_count):
+            half, row = divmod(block, ROWS)
             if filters >= LANES:
                 per = filters // LANES
                 lane = (block % per) * LANES
@@ -222,29 +246,19 @@
                 piece = jnp.concatenate(
                     [params[block * per + part, kind] for part in range(per)], axis=1
                 )
-            target[pl.ds(half * modes * ROWS + row, modes, stride=ROWS), :] = piece
+            target[pl.ds(half * mode_rows + row, modes, stride=ROWS), :] = piece
+
+    take_params(0, rates)
     decay[...] = jnp.exp(-rates[...])
-    block_decay[...] = jnp.exp(-float(length) * rates[...])
 
     def of_modes(ref, half):
-        first = half * modes * ROWS
-        return [ref[first + n * ROWS : first + (n + 1) * ROWS, :] for n in range(modes)]
-
-    def state_copy(half, step):
-        peer = lax.rem(me + step, seq_count)
-        return pltpu.make_async_remote_copy(
-            src_ref=own_state.at[half],
-            dst_ref=states.at[me, half],
-            send_sem=state_send.at[half, step],
-            recv_sem=state_recv.at[half, step],
-            device_id={"seq": peer},
-            device_id_type=MESH,
-        )
-
-    for half in range(half_count):
+        first = half * mode_rows
+        return [ref[rows_of(first + n * ROWS), :] for n in range(modes)]
+
+    def find_state(half):
         rate_of = of_modes(decay, half)
 
-        def gather_state(t, held, half=half, rate_of=rate_of):
+        def gather_state(t, held):
             value = product[rows_of(half * half_rows + t * ROWS), :]
             return [rate_of[n] * held[n] + value for n in range(modes)]
 
@@ -257,11 +271,53 @@
         )
         own_state[half] = jnp.concatenate(held, axis=0).astype(jnp.bfloat16)
 
-        def send_state(step, _, half=half):
-            state_copy(half, step).start()
+    def mate_copy(half):
+        return pltpu.make_async_remote_copy(
+            src_ref=own_state.at[half],
+            dst_ref=mate_state.at[half],
+            send_sem=mate_send.at[half],
+            recv_sem=mate_recv.at[half],
+            device_id={"seq": mate},
+            device_id_type=MESH,
+        )
+
+    find_state(1 - side)
+    mate_copy(1 - side).start()
+    block_decay[...] = jnp.exp(-float(length) * rates[...])
+    pair_decay[...] = block_decay[...] * block_decay[...]
+    find_state(side)
+
+    @pl.when(side == 0)
+    def _():
+        mate_copy(0).start()
+
+    def state_copy(later, target_side):
+        return pltpu.make_async_remote_copy(
+            src_ref=pair_state,
+            dst_ref=states.at[pair, side],
+            send_sem=state_send.at[later, target_side],
+            recv_sem=state_recv.at[pair, side],
+            device_id={"seq": 2 * later + target_side},
+            device_id_type=MESH,
+        )
+
+    def for_later(action):
+        def step(later, _):
+            for target_side in range(2):
+                action(state_copy(later, target_side))
             return 0
 
-        lax.fori_loop(1, seq_count - me, send_state, 0)
+        lax.fori_loop(pair + 1, pair_count, step, 0)
+
+    mate_copy(side).wait_recv()
+    own_part = own_state[side].astype(jnp.float32)
+    mate_part = mate_state[side].astype(jnp.float32)
+    scale = block_decay[rows_of(side * mode_rows, mode_rows), :]
+    even = jnp.where(side == 0, own_part, mate_part)
+    odd = jnp.where(side == 0, mate_part, own_part)
+    pair_state[...] = (scale * even + odd).astype(jnp.bfloat16)
+    for_later(lambda copy: copy.start())
+    take_params(1, weights)
 
     for half in range(half_count):
         rate_of = of_modes(decay, half)
@@ -278,19 +334,40 @@
             0, length, convolve, [jnp.zeros((ROWS, LANES), jnp.float32)] * modes, unroll=4
         )
 
+    def out_copy(half):
+        part = pl.ds(half * ROWS * LANES, ROWS * LANES)
+        return pltpu.make_async_copy(staged.at[part], out.at[part], out_sem.at[half])
+
+    @pl.when(side == 1)
+    def _():
+        mate_copy(0).wait_recv()
+
     for half in range(half_count):
-        mode_rows = modes * ROWS
         first = half * mode_rows
         carry[...] = jnp.zeros(carry.shape, jnp.float32)
 
         def take_state(sender, _, half=half, first=first):
-            state_copy(half, me - sender).wait_recv()
-            carry[...] = carry[...] * block_decay[first : first + mode_rows, :] + states[
+            pltpu.make_async_remote_copy(
+                src_ref=pair_state,
+                dst_ref=states.at[sender, half],
+                send_sem=state_send.at[sender, half],
+                recv_sem=state_recv.at[sender, half],
+                device_id={"seq": 2 * sender + half},
+                device_id_type=MESH,
+            ).wait_recv()
+            carry[...] = carry[...] * pair_decay[first : first + mode_rows, :] + states[
                 sender, half
             ].astype(jnp.float32)
             return 0
 
-        lax.fori_loop(0, me, take_state, 0)
+        lax.fori_loop(0, pair, take_state, 0)
+
+        @pl.when(side == 1)
+        def _(half=half, first=first):
+            carry[...] = carry[...] * block_decay[first : first + mode_rows, :] + mate_state[
+                half
+            ].astype(jnp.float32)
+
         carry[...] = carry[...] * weights[first : first + mode_rows, :]
         rate_of = of_modes(decay, half)
         skip_here = skip[half * ROWS : (half + 1) * ROWS, :]
@@ -306,12 +383,18 @@
         for row in range(ROWS):
             gated = local[pl.ds(half * half_rows + row, length, stride=ROWS), :].astype(jnp.bfloat16)
             first_channel = (half * ROWS + row) * LANES
-            out[first_channel : first_channel + LANES, :] = lax.dot_general(
+            staged[first_channel : first_channel + LANES, :] = lax.dot_general(
                 eye, gated, across, preferred_element_type=jnp.float32
             ).astype(jnp.bfloat16)
 
+        out_copy(half).start()
+
+    for half in range(half_count):
+        out_copy(half).wait()
+
     def drain_params(step, _):
-        param_copy(step).wait_send()
+        for kind in range(2):
+            param_copy(kind, step).wait_send()
         return 0
 
     lax.fori_loop(1, seq_count, drain_params, 0)
@@ -320,12 +403,13 @@
     def _():
         halo_copy.wait_send()
 
-    def drain_states(step, _):
-        for half in range(half_count):
-            state_copy(half, step).wait_send()
-        return 0
-
-    lax.fori_loop(1, seq_count - me, drain_states, 0)
+    mate_copy(1 - side).wait_send()
+
+    @pl.when(side == 0)
+    def _():
+        mate_copy(0).wait_send()
+
+    for_later(lambda copy: copy.wait_send())
 
 
 def tree_sum(terms):
@@ -340,18 +424,20 @@
     filters, modes = residue.shape
     block_count = width // LANES
     half_count = block_count // ROWS
+    assert half_count == 2 and seq_count % 2 == 0
     call = functools.partial(kernel, seq_count, modes, half_count, length, filters)
-    vmem = pl.BlockSpec(memory_space=pltpu.VMEM)
-    anywhere = pl.BlockSpec(memory_space=pl.ANY)
+    hbm = pl.BlockSpec(memory_space=pltpu.HBM)
     mode_rows = modes * ROWS
     f32, bf16 = jnp.float32, jnp.bfloat16
     dma = pltpu.SemaphoreType.DMA
     return pl.pallas_call(
         call,
         out_shape=jax.ShapeDtypeStruct((width, length), bf16),
-        in_specs=[anywhere, anywhere, anywhere, vmem, vmem],
-        out_specs=vmem,
+        in_specs=[hbm] * 5,
+        out_specs=hbm,
         scratch_shapes=[
+            pltpu.VMEM((modes, filters), f32),
+            pltpu.VMEM((modes, filters), f32),
             pltpu.VMEM((3, width, length), bf16),
             pltpu.VMEM((3, 3, width), f32),
             pltpu.VMEM((block_count, LANES), f32),
@@ -366,22 +452,29 @@
             pltpu.VMEM((half_count * mode_rows, LANES), f32),
             pltpu.VMEM((half_count * mode_rows, LANES), f32),
             pltpu.VMEM((half_count * mode_rows, LANES), f32),
+            pltpu.VMEM((half_count * mode_rows, LANES), f32),
             pltpu.VMEM((6, block_count, LANES), bf16),
             pltpu.VMEM((6, block_count, LANES), bf16),
             pltpu.VMEM((half_count, mode_rows, LANES), bf16),
-            pltpu.VMEM((seq_count, half_count, mode_rows, LANES), bf16),
+            pltpu.VMEM((half_count, mode_rows, LANES), bf16),
+            pltpu.VMEM((mode_rows, LANES), bf16),
+            pltpu.VMEM((seq_count // 2, half_count, mode_rows, LANES), bf16),
             pltpu.VMEM((mode_rows, LANES), f32),
+            pltpu.VMEM((width, length), bf16),
             dma((3,)),
             dma((2,)),
-            dma((seq_count,)),
-            dma((seq_count,)),
+            dma((4,)),
+            dma((2, seq_count)),
+            dma((2, seq_count)),
             dma,
             dma,
-            dma((half_count, seq_count)),
-            dma((half_count, seq_count)),
+            dma((2,)),
+            dma((2,)),
+            dma((seq_count // 2, 2)),
+            dma((seq_count // 2, 2)),
         ],
         compiler_params=pltpu.CompilerParams(
-            collective_id=0, has_side_effects=True, vmem_limit_bytes=40 * 1024 * 1024
+            collective_id=0, has_side_effects=True, vmem_limit_bytes=60 * 1024 * 1024
         ),
     )(
         projected,

time: 22.7 us -> 17.5 us (0.77)
  the two profiles are of different devices: /device:TPU:5 before, /device:TPU:15 now
where the time goes in v1:
time: 17.5 us; the launch traced here: 17.3 us
  Pallas kernels  15.4 us (88%)
  local copies, waits for them, and re-layouts  1.87 us (11%)
    pallas_call x1, Pallas kernels, body(): pl.pallas_call(call, out_shape=jax.ShapeDtypeStruct((width, length), bf16...  15.4 us
    unnamed x1, local copies, waits for them, and re-layouts  1.87 us

profile of v1, /device:TPU:15, one launch (start us, length us, event | category | flops | bytes accessed | tf_op | source)
XLA Modules:
  0.0 17.3 jit_solution(8255283343575458593)
XLA Ops:
  0.0 15.4 %shard_map.55 = bf16[2048,128]{1,0:T(8,128)(2,1)} custom-call(bf16[3,2048,128]{2,1,0:T(8,128)(2,1)} %projected.1, f32[3,3,8192]{2,1,0:T(4,128)} %taps_hbm.1, f32[64,128]{1,0:T(8,128)} %bitcast.3, f32[16,256]{1,0:T(8,128)} %bitcast.4, f32[16,256]{1,0:T(8,128)} %bitcast.5), custom_call_target="tpu_custom_call" | custom-call | tf_op jit(solution)/shard_map/pallas_call | solution.py:433
  15.4 1.9 %copy.7 = bf16[2048,128]{1,0:T(8,128)(2,1)} copy(bf16[2048,128]{1,0:T(8,128)(2,1)} %shard_map.55) | data formatting | bytes 1048576

commit v2 on v1

--- a/solution.py
+++ b/solution.py
@@ -52,9 +52,7 @@
     pair_state,
     states,
     carry,
-    staged,
     in_sem,
-    out_sem,
     tap_sem,
     param_send,
     param_recv,
@@ -131,25 +129,13 @@
 
     send_params(0)
 
-    eye = (
-        lax.broadcasted_iota(jnp.int32, (LANES, LANES), 0)
-        == lax.broadcasted_iota(jnp.int32, (LANES, LANES), 1)
-    ).astype(jnp.bfloat16)
-    across = (((1,), (1,)), ((), ()))
     for s in range(3):
         in_copies[s].wait()
-        for couple in range(block_count // 2):
-            turned = lax.dot_general(
-                eye,
-                streams[s, couple * 256 : couple * 256 + 256, :],
-                across,
-                preferred_element_type=jnp.float32,
+        for block in range(block_count):
+            half, row = divmod(block, ROWS)
+            laid[pl.ds((s * half_count + half) * half_rows + row, length, stride=ROWS), :] = (
+                streams[s, block * LANES : (block + 1) * LANES, :].T.astype(jnp.float32)
             )
-            for part in range(2):
-                half, row = divmod(couple * 2 + part, ROWS)
-                laid[pl.ds((s * half_count + half) * half_rows + row, length, stride=ROWS), :] = (
-                    turned[:, part * LANES : (part + 1) * LANES]
-                )
 
     def laid_row(s, half, t):
         return laid[rows_of((s * half_count + half) * half_rows + t * ROWS), :]
@@ -334,10 +320,6 @@
             0, length, convolve, [jnp.zeros((ROWS, LANES), jnp.float32)] * modes, unroll=4
         )
 
-    def out_copy(half):
-        part = pl.ds(half * ROWS * LANES, ROWS * LANES)
-        return pltpu.make_async_copy(staged.at[part], out.at[part], out_sem.at[half])
-
     @pl.when(side == 1)
     def _():
         mate_copy(0).wait_recv()
@@ -383,14 +365,8 @@
         for row in range(ROWS):
             gated = local[pl.ds(half * half_rows + row, length, stride=ROWS), :].astype(jnp.bfloat16)
             first_channel = (half * ROWS + row) * LANES
-            staged[first_channel : first_channel + LANES, :] = lax.dot_general(
-                eye, gated, across, preferred_element_type=jnp.float32
-            ).astype(jnp.bfloat16)
-
-        out_copy(half).start()
-
-    for half in range(half_count):
-        out_copy(half).wait()
+            out[first_channel : first_channel + LANES, :] = gated.T
+
 
     def drain_params(step, _):
         for kind in range(2):
@@ -432,9 +408,9 @@
     dma = pltpu.SemaphoreType.DMA
     return pl.pallas_call(
         call,
-        out_shape=jax.ShapeDtypeStruct((width, length), bf16),
+        out_shape=pltpu.VMEM((width, length), bf16),
         in_specs=[hbm] * 5,
-        out_specs=hbm,
+        out_specs=pl.BlockSpec(memory_space=pltpu.VMEM),
         scratch_shapes=[
             pltpu.VMEM((modes, filters), f32),
             pltpu.VMEM((modes, filters), f32),
@@ -460,9 +436,7 @@
             pltpu.VMEM((mode_rows, LANES), bf16),
             pltpu.VMEM((seq_count // 2, half_count, mode_rows, LANES), bf16),
             pltpu.VMEM((mode_rows, LANES), f32),
-            pltpu.VMEM((width, length), bf16),
             dma((3,)),
-            dma((2,)),
             dma((4,)),
             dma((2, seq_count)),
             dma((2, seq_count)),

time: 17.5 us -> 15.4 us (0.88)
  the two profiles are of different devices: /device:TPU:15 before, /device:TPU:5 now
where the time goes in v2:
time: 15.4 us; the launch traced here: 15.2 us
  Pallas kernels  14.4 us (94%)
  local copies, waits for them, and re-layouts  0.8 us (5%)
    pallas_call x1, Pallas kernels, body(): pl.pallas_call(call, out_shape=pltpu.VMEM((width, length), bf16), in_spec...  14.4 us
    unnamed x1, local copies, waits for them, and re-layouts  0.8 us

profile of v2, /device:TPU:5, one launch (start us, length us, event | category | flops | bytes accessed | tf_op | source)
XLA Modules:
  0.0 15.2 jit_solution(12170371758630316284)
XLA Ops:
  0.0 14.4 %shard_map.55 = bf16[2048,128]{1,0:T(8,128)(2,1)S(1)} custom-call(bf16[3,2048,128]{2,1,0:T(8,128)(2,1)} %projected.1, f32[3,3,8192]{2,1,0:T(4,128)} %taps_hbm.1, f32[64,128]{1,0:T(8,128)} %bitcast.3, f32[16,256]{1,0:T(8,128)} %bitcast.4, f32[16,256]{1,0:T(8,128)} %bitcast.5), custom_call_target="tpu_custom_call" | custom-call | tf_op jit(solution)/shard_map/pallas_call | solution.py:409
  14.4 0.8 %copy.7 = bf16[2048,128]{1,0:T(8,128)(2,1)} copy(bf16[2048,128]{1,0:T(8,128)(2,1)S(1)} %shard_map.55) | data formatting | bytes 1048576

commit v3 on v2

--- a/solution.py
+++ b/solution.py
@@ -52,6 +52,8 @@
     pair_state,
     states,
     carry,
+    prefix,
+    mate_prefix,
     in_sem,
     tap_sem,
     param_send,
@@ -62,6 +64,8 @@
     mate_recv,
     state_send,
     state_recv,
+    prefix_send,
+    prefix_recv,
 ):
     me = lax.axis_index("seq")
     group = lax.axis_index("mp")
@@ -89,10 +93,18 @@
     residue_copy = pltpu.make_async_copy(residue_hbm, residue, tap_sem.at[3])
     rate_copy.start()
     residue_copy.start()
-    for copy in in_copies:
-        copy.start()
+    for s in (1, 2, 0):
+        in_copies[s].start()
     tap_copy.start()
     skip_copy.start()
+
+    def turn(s):
+        in_copies[s].wait()
+        for block in range(block_count):
+            half, row = divmod(block, ROWS)
+            laid[pl.ds((s * half_count + half) * half_rows + row, length, stride=ROWS), :] = (
+                streams[s, block * LANES : (block + 1) * LANES, :].T.astype(jnp.float32)
+            )
 
     barrier = pltpu.get_barrier_semaphore()
 
@@ -107,6 +119,7 @@
     own_params[0] = rate[...]
     own_params[1] = residue[...] * jnp.sqrt(rate[...])
     params[me] = own_params[...]
+    turn(1)
     pl.semaphore_wait(barrier, seq_count - 1)
 
     def param_copy(kind, step):
@@ -129,35 +142,41 @@
 
     send_params(0)
 
-    for s in range(3):
-        in_copies[s].wait()
-        for block in range(block_count):
-            half, row = divmod(block, ROWS)
-            laid[pl.ds((s * half_count + half) * half_rows + row, length, stride=ROWS), :] = (
-                streams[s, block * LANES : (block + 1) * LANES, :].T.astype(jnp.float32)
-            )
-
     def laid_row(s, half, t):
         return laid[rows_of((s * half_count + half) * half_rows + t * ROWS), :]
 
-    for s in range(3):
+    turn(2)
+
+    def halo_copy(s):
+        return pltpu.make_async_remote_copy(
+            src_ref=halo_out.at[s],
+            dst_ref=halo_in.at[s],
+            send_sem=halo_send.at[s],
+            recv_sem=halo_recv.at[s],
+            device_id={"seq": lax.rem(me + 1, seq_count)},
+            device_id_type=MESH,
+        )
+
+    def send_halo(s):
         for back in range(2):
             pieces = [laid_row(s, half, length - 2 + back) for half in range(half_count)]
-            halo_out[s * 2 + back] = jnp.concatenate(pieces, axis=0).astype(jnp.bfloat16)
-
-    halo_copy = pltpu.make_async_remote_copy(
-        src_ref=halo_out,
-        dst_ref=halo_in,
-        send_sem=halo_send,
-        recv_sem=halo_recv,
-        device_id={"seq": lax.rem(me + 1, seq_count)},
-        device_id_type=MESH,
-    )
-
-    @pl.when(me < seq_count - 1)
-    def _():
-        halo_copy.start()
-
+            halo_out[s, back] = jnp.concatenate(pieces, axis=0).astype(jnp.bfloat16)
+
+        @pl.when(me < seq_count - 1)
+        def _():
+            halo_copy(s).start()
+
+    def take_halo(s):
+        @pl.when(me > 0)
+        def _():
+            halo_copy(s).wait_recv()
+
+        @pl.when(me == 0)
+        def _():
+            halo_in[s] = jnp.zeros(halo_in.shape[1:], halo_in.dtype)
+
+    send_halo(1)
+    send_halo(2)
     send_params(1)
     tap_copy.wait()
     skip_copy.wait()
@@ -168,52 +187,56 @@
                     lag, s : s + 1, block * LANES : (block + 1) * LANES
                 ]
 
-    def tap_rows(half):
-        return [
-            [taps[lag * 3 + s, half * ROWS : (half + 1) * ROWS, :] for lag in range(3)]
-            for s in range(3)
+    def mix_streams(which, put):
+        taps_of = [
+            [
+                [taps[lag * 3 + s, half * ROWS : (half + 1) * ROWS, :] for lag in range(3)]
+                for s in which
+            ]
+            for half in range(half_count)
         ]
 
-    def put_mixed(half, t, now, before, earlier, tap):
-        q, k, v = [
-            tap[s][0] * now[s] + tap[s][1] * before[s] + tap[s][2] * earlier[s] for s in range(3)
-        ]
-        at = rows_of(half * half_rows + t * ROWS)
-        mixed_q[at, :] = q
-        product[at, :] = (k * v).astype(jnp.bfloat16).astype(jnp.float32)
-
-    for half in range(half_count):
-        tap = tap_rows(half)
-
-        def mix(t, past, half=half, tap=tap):
-            before, earlier = past
-            now = [laid_row(s, half, t) for s in range(3)]
-            put_mixed(half, t, now, before, earlier, tap)
-            return now, before
-
-        first = [[laid_row(s, half, t) for s in range(3)] for t in range(2)]
-        lax.fori_loop(2, length, mix, (first[1], first[0]), unroll=6)
-
-    @pl.when(me > 0)
-    def _():
-        halo_copy.wait_recv()
-
-    @pl.when(me == 0)
-    def _():
-        halo_in[...] = jnp.zeros(halo_in.shape, halo_in.dtype)
-
-    for half in range(half_count):
-        tap = tap_rows(half)
-        past = [
-            [
-                halo_in[s * 2 + back].astype(jnp.float32)[half * ROWS : (half + 1) * ROWS]
-                for s in range(3)
+        def mix_at(half, t, now, before, earlier):
+            put(
+                rows_of(half * half_rows + t * ROWS),
+                [
+                    tap[0] * now[i] + tap[1] * before[i] + tap[2] * earlier[i]
+                    for i, tap in enumerate(taps_of[half])
+                ],
+            )
+
+        for half in range(half_count):
+
+            def mix(t, past, half=half):
+                before, earlier = past
+                now = [laid_row(s, half, t) for s in which]
+                mix_at(half, t, now, before, earlier)
+                return now, before
+
+            first = [[laid_row(s, half, t) for s in which] for t in range(2)]
+            lax.fori_loop(2, length, mix, (first[1], first[0]), unroll=6)
+
+        for s in which:
+            take_halo(s)
+        for half in range(half_count):
+            past = [
+                [
+                    halo_in[s, back].astype(jnp.float32)[half * ROWS : (half + 1) * ROWS]
+                    for s in which
+                ]
+                for back in range(2)
             ]
-            for back in range(2)
-        ]
-        first = [[laid_row(s, half, t) for s in range(3)] for t in range(2)]
-        put_mixed(half, 0, first[0], past[1], past[0], tap)
-        put_mixed(half, 1, first[1], first[0], past[1], tap)
+            first = [[laid_row(s, half, t) for s in which] for t in range(2)]
+            mix_at(half, 0, first[0], past[1], past[0])
+            mix_at(half, 1, first[1], first[0], past[1])
+
+    def put_product(at, mixed):
+        product[at, :] = (mixed[0] * mixed[1]).astype(jnp.bfloat16).astype(jnp.float32)
+
+    def put_q(at, mixed):
+        mixed_q[at, :] = mixed[0]
+
+    mix_streams((1, 2), put_product)
 
     def take_params(kind, target):
         def take(step, _):
@@ -277,20 +300,19 @@
     def _():
         mate_copy(0).start()
 
-    def state_copy(later, target_side):
+    def state_copy(sender, later):
         return pltpu.make_async_remote_copy(
             src_ref=pair_state,
-            dst_ref=states.at[pair, side],
-            send_sem=state_send.at[later, target_side],
-            recv_sem=state_recv.at[pair, side],
-            device_id={"seq": 2 * later + target_side},
+            dst_ref=states.at[sender],
+            send_sem=state_send.at[later],
+            recv_sem=state_recv.at[sender],
+            device_id={"seq": 2 * later + side},
             device_id_type=MESH,
         )
 
     def for_later(action):
         def step(later, _):
-            for target_side in range(2):
-                action(state_copy(later, target_side))
+            action(state_copy(pair, later))
             return 0
 
         lax.fori_loop(pair + 1, pair_count, step, 0)
@@ -303,6 +325,8 @@
     odd = jnp.where(side == 0, mate_part, own_part)
     pair_state[...] = (scale * even + odd).astype(jnp.bfloat16)
     for_later(lambda copy: copy.start())
+    turn(0)
+    send_halo(0)
     take_params(1, weights)
 
     for half in range(half_count):
@@ -320,39 +344,58 @@
             0, length, convolve, [jnp.zeros((ROWS, LANES), jnp.float32)] * modes, unroll=4
         )
 
+    prefix_copy = pltpu.make_async_remote_copy(
+        src_ref=prefix,
+        dst_ref=mate_prefix,
+        send_sem=prefix_send,
+        recv_sem=prefix_recv,
+        device_id={"seq": mate},
+        device_id_type=MESH,
+    )
+    prefix[...] = jnp.zeros(prefix.shape, jnp.float32)
+
+    def take_state(sender, _):
+        state_copy(sender, sender).wait_recv()
+        prefix[...] = prefix[...] * pair_decay[rows_of(side * mode_rows, mode_rows), :] + states[
+            sender
+        ].astype(jnp.float32)
+        return 0
+
+    lax.fori_loop(0, pair, take_state, 0)
+
+    @pl.when(pair > 0)
+    def _():
+        prefix_copy.start()
+
+    mix_streams((0,), put_q)
+
     @pl.when(side == 1)
     def _():
         mate_copy(0).wait_recv()
 
-    for half in range(half_count):
-        first = half * mode_rows
-        carry[...] = jnp.zeros(carry.shape, jnp.float32)
-
-        def take_state(sender, _, half=half, first=first):
-            pltpu.make_async_remote_copy(
-                src_ref=pair_state,
-                dst_ref=states.at[sender, half],
-                send_sem=state_send.at[sender, half],
-                recv_sem=state_recv.at[sender, half],
-                device_id={"seq": 2 * sender + half},
-                device_id_type=MESH,
-            ).wait_recv()
-            carry[...] = carry[...] * pair_decay[first : first + mode_rows, :] + states[
-                sender, half
-            ].astype(jnp.float32)
-            return 0
-
-        lax.fori_loop(0, pair, take_state, 0)
+    for turn_at in range(2):
+        half = side if turn_at == 0 else 1 - side
+        here = rows_of(half * mode_rows, mode_rows)
+        if turn_at == 0:
+            carry[...] = prefix[...]
+        else:
+
+            @pl.when(pair > 0)
+            def _():
+                prefix_copy.wait_recv()
+                carry[...] = mate_prefix[...]
+
+            @pl.when(pair == 0)
+            def _():
+                carry[...] = jnp.zeros(carry.shape, jnp.float32)
 
         @pl.when(side == 1)
-        def _(half=half, first=first):
-            carry[...] = carry[...] * block_decay[first : first + mode_rows, :] + mate_state[
-                half
-            ].astype(jnp.float32)
-
-        carry[...] = carry[...] * weights[first : first + mode_rows, :]
+        def _(half=half, here=here):
+            carry[...] = carry[...] * block_decay[here, :] + mate_state[half].astype(jnp.float32)
+
+        carry[...] = carry[...] * weights[here, :]
         rate_of = of_modes(decay, half)
-        skip_here = skip[half * ROWS : (half + 1) * ROWS, :]
+        skip_here = skip[rows_of(half * ROWS), :]
 
         def finish(t, held, half=half, rate_of=rate_of, skip_here=skip_here):
             at = rows_of(half * half_rows + t * ROWS)
@@ -364,8 +407,8 @@
         lax.fori_loop(0, length, finish, of_modes(carry, 0), unroll=4)
         for row in range(ROWS):
             gated = local[pl.ds(half * half_rows + row, length, stride=ROWS), :].astype(jnp.bfloat16)
-            first_channel = (half * ROWS + row) * LANES
-            out[first_channel : first_channel + LANES, :] = gated.T
+            first_channel = pl.multiple_of((half * ROWS + row) * LANES, LANES)
+            out[pl.ds(first_channel, LANES), :] = gated.T
 
 
     def drain_params(step, _):
@@ -377,7 +420,8 @@
 
     @pl.when(me < seq_count - 1)
     def _():
-        halo_copy.wait_send()
+        for s in range(3):
+            halo_copy(s).wait_send()
 
     mate_copy(1 - side).wait_send()
 
@@ -386,6 +430,10 @@
         mate_copy(0).wait_send()
 
     for_later(lambda copy: copy.wait_send())
+
+    @pl.when(pair > 0)
+    def _():
+        prefix_copy.wait_send()
 
 
 def tree_sum(terms):
@@ -429,23 +477,27 @@
             pltpu.VMEM((half_count * mode_rows, LANES), f32),
             pltpu.VMEM((half_count * mode_rows, LANES), f32),
             pltpu.VMEM((half_count * mode_rows, LANES), f32),
-            pltpu.VMEM((6, block_count, LANES), bf16),
-            pltpu.VMEM((6, block_count, LANES), bf16),
+            pltpu.VMEM((3, 2, block_count, LANES), bf16),
+            pltpu.VMEM((3, 2, block_count, LANES), bf16),
             pltpu.VMEM((half_count, mode_rows, LANES), bf16),
             pltpu.VMEM((half_count, mode_rows, LANES), bf16),
             pltpu.VMEM((mode_rows, LANES), bf16),
-            pltpu.VMEM((seq_count // 2, half_count, mode_rows, LANES), bf16),
+            pltpu.VMEM((seq_count // 2, mode_rows, LANES), bf16),
+            pltpu.VMEM((mode_rows, LANES), f32),
+            pltpu.VMEM((mode_rows, LANES), f32),
             pltpu.VMEM((mode_rows, LANES), f32),
             dma((3,)),
             dma((4,)),
             dma((2, seq_count)),
             dma((2, seq_count)),
+            dma((3,)),
+            dma((3,)),
+            dma((2,)),
+            dma((2,)),
+            dma((seq_count // 2,)),
+            dma((seq_count // 2,)),
             dma,
             dma,
-            dma((2,)),
-            dma((2,)),
-            dma((seq_count // 2, 2)),
-            dma((seq_count // 2, 2)),
         ],
         compiler_params=pltpu.CompilerParams(
             collective_id=0, has_side_effects=True, vmem_limit_bytes=60 * 1024 * 1024

time: 15.4 us -> 15.8 us (1.026)
  the two profiles are of different devices: /device:TPU:5 before, /device:TPU:0 now
where the time goes in v3:
time: 15.8 us; the launch traced here: 15.5 us
  Pallas kernels  14.7 us (93%)
  local copies, waits for them, and re-layouts  0.8 us (5%)
    pallas_call x1, Pallas kernels, body(): pl.pallas_call(call, out_shape=pltpu.VMEM((width, length), bf16), in_spec...  14.7 us
    unnamed x1, local copies, waits for them, and re-layouts  0.8 us

profile of v3, /device:TPU:0, one launch (start us, length us, event | category | flops | bytes accessed | tf_op | source)
XLA Modules:
  0.0 15.5 jit_solution(9608873906926389191)
XLA Ops:
  0.0 14.7 %shard_map.55 = bf16[2048,128]{1,0:T(8,128)(2,1)S(1)} custom-call(bf16[3,2048,128]{2,1,0:T(8,128)(2,1)} %projected.1, f32[3,3,8192]{2,1,0:T(4,128)} %taps_hbm.1, f32[64,128]{1,0:T(8,128)} %bitcast.3, f32[16,256]{1,0:T(8,128)} %bitcast.4, f32[16,256]{1,0:T(8,128)} %bitcast.5), custom_call_target="tpu_custom_call" | custom-call | tf_op jit(solution)/shard_map/pallas_call | solution.py:457
  14.7 0.8 %copy.7 = bf16[2048,128]{1,0:T(8,128)(2,1)} copy(bf16[2048,128]{1,0:T(8,128)(2,1)S(1)} %shard_map.55) | data formatting | bytes 1048576

commit v4 on v3

--- a/solution.py
+++ b/solution.py
@@ -52,6 +52,7 @@
     pair_state,
     states,
     carry,
+    start,
     prefix,
     mate_prefix,
     in_sem,
@@ -177,6 +178,8 @@
 
     send_halo(1)
     send_halo(2)
+    turn(0)
+    send_halo(0)
     send_params(1)
     tap_copy.wait()
     skip_copy.wait()
@@ -325,9 +328,20 @@
     odd = jnp.where(side == 0, mate_part, own_part)
     pair_state[...] = (scale * even + odd).astype(jnp.bfloat16)
     for_later(lambda copy: copy.start())
-    turn(0)
-    send_halo(0)
+    mix_streams((0,), put_q)
     take_params(1, weights)
+
+    @pl.when(side == 1)
+    def _():
+        mate_copy(0).wait_recv()
+        for half in range(half_count):
+            start[half * mode_rows : (half + 1) * mode_rows, :] = mate_state[half].astype(
+                jnp.float32
+            )
+
+    @pl.when(side == 0)
+    def _():
+        start[...] = jnp.zeros(start.shape, jnp.float32)
 
     for half in range(half_count):
         rate_of = of_modes(decay, half)
@@ -340,9 +354,7 @@
             local[at, :] = tree_sum([weight_of[n] * held[n] for n in range(modes)])
             return held
 
-        lax.fori_loop(
-            0, length, convolve, [jnp.zeros((ROWS, LANES), jnp.float32)] * modes, unroll=4
-        )
+        lax.fori_loop(0, length, convolve, of_modes(start, half), unroll=4)
 
     prefix_copy = pltpu.make_async_remote_copy(
         src_ref=prefix,
@@ -367,49 +379,55 @@
     def _():
         prefix_copy.start()
 
-    mix_streams((0,), put_q)
-
-    @pl.when(side == 1)
-    def _():
-        mate_copy(0).wait_recv()
-
-    for turn_at in range(2):
-        half = side if turn_at == 0 else 1 - side
-        here = rows_of(half * mode_rows, mode_rows)
-        if turn_at == 0:
-            carry[...] = prefix[...]
-        else:
-
-            @pl.when(pair > 0)
-            def _():
-                prefix_copy.wait_recv()
-                carry[...] = mate_prefix[...]
-
-            @pl.when(pair == 0)
-            def _():
-                carry[...] = jnp.zeros(carry.shape, jnp.float32)
-
-        @pl.when(side == 1)
-        def _(half=half, here=here):
-            carry[...] = carry[...] * block_decay[here, :] + mate_state[half].astype(jnp.float32)
-
-        carry[...] = carry[...] * weights[here, :]
-        rate_of = of_modes(decay, half)
-        skip_here = skip[rows_of(half * ROWS), :]
-
-        def finish(t, held, half=half, rate_of=rate_of, skip_here=skip_here):
-            at = rows_of(half * half_rows + t * ROWS)
-            held = [rate_of[n] * held[n] for n in range(modes)]
-            long_part = (local[at, :] + tree_sum(held)).astype(jnp.bfloat16).astype(jnp.float32)
-            local[at, :] = mixed_q[at, :] * (long_part + skip_here * product[at, :])
-            return held
-
-        lax.fori_loop(0, length, finish, of_modes(carry, 0), unroll=4)
+    def put_gated(at, skip_here, long_part):
+        long_part = long_part.astype(jnp.bfloat16).astype(jnp.float32)
+        local[at, :] = mixed_q[at, :] * (long_part + skip_here * product[at, :])
+
+    def put_out(half):
         for row in range(ROWS):
             gated = local[pl.ds(half * half_rows + row, length, stride=ROWS), :].astype(jnp.bfloat16)
             first_channel = pl.multiple_of((half * ROWS + row) * LANES, LANES)
             out[pl.ds(first_channel, LANES), :] = gated.T
 
+    @pl.when(pair == 0)
+    def _():
+        for half in range(half_count):
+            skip_here = skip[rows_of(half * ROWS), :]
+
+            def finish(t, _, half=half, skip_here=skip_here):
+                at = rows_of(half * half_rows + t * ROWS)
+                put_gated(at, skip_here, local[at, :])
+                return 0
+
+            lax.fori_loop(0, length, finish, 0, unroll=8)
+            put_out(half)
+
+    @pl.when(pair > 0)
+    def _():
+        for order in range(2):
+            half = side if order == 0 else 1 - side
+            here = rows_of(half * mode_rows, mode_rows)
+            if order == 0:
+                carry[...] = prefix[...] * weights[here, :]
+            else:
+                prefix_copy.wait_recv()
+                carry[...] = mate_prefix[...] * weights[here, :]
+
+            @pl.when(side == 1)
+            def _(here=here):
+                carry[...] = carry[...] * block_decay[here, :]
+
+            rate_of = of_modes(decay, half)
+            skip_here = skip[rows_of(half * ROWS), :]
+
+            def finish(t, held, half=half, rate_of=rate_of, skip_here=skip_here):
+                at = rows_of(half * half_rows + t * ROWS)
+                held = [rate_of[n] * held[n] for n in range(modes)]
+                put_gated(at, skip_here, local[at, :] + tree_sum(held))
+                return held
+
+            lax.fori_loop(0, length, finish, of_modes(carry, 0), unroll=4)
+            put_out(half)
 
     def drain_params(step, _):
         for kind in range(2):
@@ -484,6 +502,7 @@
             pltpu.VMEM((mode_rows, LANES), bf16),
             pltpu.VMEM((seq_count // 2, mode_rows, LANES), bf16),
             pltpu.VMEM((mode_rows, LANES), f32),
+            pltpu.VMEM((half_count * mode_rows, LANES), f32),
             pltpu.VMEM((mode_rows, LANES), f32),
             pltpu.VMEM((mode_rows, LANES), f32),
             dma((3,)),

time: 15.8 us -> 14.8 us (0.937)
  the two profiles are of different devices: /device:TPU:0 before, /device:TPU:5 now
where the time goes in v4:
time: 14.8 us; the launch traced here: 14.6 us
  Pallas kernels  13.7 us (93%)
  local copies, waits for them, and re-layouts  0.8 us (5%)
    pallas_call x1, Pallas kernels, body(): pl.pallas_call(call, out_shape=pltpu.VMEM((width, length), bf16), in_spec...  13.7 us
    unnamed x1, local copies, waits for them, and re-layouts  0.8 us

profile of v4, /device:TPU:5, one launch (start us, length us, event | category | flops | bytes accessed | tf_op | source)
XLA Modules:
  0.0 14.6 jit_solution(15660225796061356329)
XLA Ops:
  0.0 13.7 %shard_map.55 = bf16[2048,128]{1,0:T(8,128)(2,1)S(1)} custom-call(bf16[3,2048,128]{2,1,0:T(8,128)(2,1)} %projected.1, f32[3,3,8192]{2,1,0:T(4,128)} %taps_hbm.1, f32[64,128]{1,0:T(8,128)} %bitcast.3, f32[16,256]{1,0:T(8,128)} %bitcast.4, f32[16,256]{1,0:T(8,128)} %bitcast.5), custom_call_target="tpu_custom_call" | custom-call | tf_op jit(solution)/shard_map/pallas_call | solution.py:475
  13.8 0.8 %copy.7 = bf16[2048,128]{1,0:T(8,128)(2,1)} copy(bf16[2048,128]{1,0:T(8,128)(2,1)S(1)} %shard_map.55) | data formatting | bytes 1048576

commit v5 on v4

--- a/solution.py
+++ b/solution.py
@@ -320,6 +320,7 @@
 
         lax.fori_loop(pair + 1, pair_count, step, 0)
 
+    mix_streams((0,), put_q)
     mate_copy(side).wait_recv()
     own_part = own_state[side].astype(jnp.float32)
     mate_part = mate_state[side].astype(jnp.float32)
@@ -328,22 +329,17 @@
     odd = jnp.where(side == 0, mate_part, own_part)
     pair_state[...] = (scale * even + odd).astype(jnp.bfloat16)
     for_later(lambda copy: copy.start())
-    mix_streams((0,), put_q)
     take_params(1, weights)
 
-    @pl.when(side == 1)
-    def _():
-        mate_copy(0).wait_recv()
-        for half in range(half_count):
-            start[half * mode_rows : (half + 1) * mode_rows, :] = mate_state[half].astype(
-                jnp.float32
-            )
-
-    @pl.when(side == 0)
-    def _():
-        start[...] = jnp.zeros(start.shape, jnp.float32)
-
-    for half in range(half_count):
+    start[...] = jnp.zeros(start.shape, jnp.float32)
+    for half in (1, 0):
+
+        @pl.when(side == 1)
+        def _(half=half):
+            if half == 0:
+                mate_copy(0).wait_recv()
+            start[...] = mate_state[half].astype(jnp.float32)
+
         rate_of = of_modes(decay, half)
         weight_of = of_modes(weights, half)
 
@@ -354,7 +350,7 @@
             local[at, :] = tree_sum([weight_of[n] * held[n] for n in range(modes)])
             return held
 
-        lax.fori_loop(0, length, convolve, of_modes(start, half), unroll=4)
+        lax.fori_loop(0, length, convolve, of_modes(start, 0), unroll=4)
 
     prefix_copy = pltpu.make_async_remote_copy(
         src_ref=prefix,
@@ -383,11 +379,12 @@
         long_part = long_part.astype(jnp.bfloat16).astype(jnp.float32)
         local[at, :] = mixed_q[at, :] * (long_part + skip_here * product[at, :])
 
-    def put_out(half):
-        for row in range(ROWS):
-            gated = local[pl.ds(half * half_rows + row, length, stride=ROWS), :].astype(jnp.bfloat16)
-            first_channel = pl.multiple_of((half * ROWS + row) * LANES, LANES)
-            out[pl.ds(first_channel, LANES), :] = gated.T
+    def gated_of(half, row):
+        return local[pl.ds(half * half_rows + row, length, stride=ROWS), :].astype(jnp.bfloat16)
+
+    def put_out(half, row, gated):
+        first_channel = pl.multiple_of((half * ROWS + row) * LANES, LANES)
+        out[pl.ds(first_channel, LANES), :] = gated.T
 
     @pl.when(pair == 0)
     def _():
@@ -400,7 +397,8 @@
                 return 0
 
             lax.fori_loop(0, length, finish, 0, unroll=8)
-            put_out(half)
+            for row in range(ROWS):
+                put_out(half, row, gated_of(half, row))
 
     @pl.when(pair > 0)
     def _():
@@ -426,8 +424,20 @@
                 put_gated(at, skip_here, local[at, :] + tree_sum(held))
                 return held
 
-            lax.fori_loop(0, length, finish, of_modes(carry, 0), unroll=4)
-            put_out(half)
+            if order == 0:
+                lax.fori_loop(0, length, finish, of_modes(carry, 0), unroll=4)
+                continue
+
+            def finish_some(row, held, finish=finish):
+                gated = gated_of(side, row)
+                for step in range(length // ROWS):
+                    held = finish(row * (length // ROWS) + step, held)
+                put_out(side, row, gated)
+                return held
+
+            lax.fori_loop(0, ROWS, finish_some, of_modes(carry, 0))
+            for row in range(ROWS):
+                put_out(half, row, gated_of(half, row))
 
     def drain_params(step, _):
         for kind in range(2):
@@ -502,7 +512,7 @@
             pltpu.VMEM((mode_rows, LANES), bf16),
             pltpu.VMEM((seq_count // 2, mode_rows, LANES), bf16),
             pltpu.VMEM((mode_rows, LANES), f32),
-            pltpu.VMEM((half_count * mode_rows, LANES), f32),
+            pltpu.VMEM((mode_rows, LANES), f32),
             pltpu.VMEM((mode_rows, LANES), f32),
             pltpu.VMEM((mode_rows, LANES), f32),
             dma((3,)),

time: 14.8 us -> 14.9 us (level)
  Pallas kernels: 13.7 us -> 13.9 us
where the time goes in v5:
time: 14.9 us; the launch traced here: 14.7 us
  Pallas kernels  13.9 us (93%)
  local copies, waits for them, and re-layouts  0.8 us (5%)
    pallas_call x1, Pallas kernels, body(): pl.pallas_call(call, out_shape=pltpu.VMEM((width, length), bf16), in_spec...  13.9 us
    unnamed x1, local copies, waits for them, and re-layouts  0.8 us

profile of v5, /device:TPU:5, one launch (start us, length us, event | category | flops | bytes accessed | tf_op | source)
XLA Modules:
  0.0 14.7 jit_solution(18199656697963656901)
XLA Ops:
  0.0 13.9 %shard_map.55 = bf16[2048,128]{1,0:T(8,128)(2,1)S(1)} custom-call(bf16[3,2048,128]{2,1,0:T(8,128)(2,1)} %projected.1, f32[3,3,8192]{2,1,0:T(4,128)} %taps_hbm.1, f32[64,128]{1,0:T(8,128)} %bitcast.3, f32[16,256]{1,0:T(8,128)} %bitcast.4, f32[16,256]{1,0:T(8,128)} %bitcast.5), custom_call_target="tpu_custom_call" | custom-call | tf_op jit(solution)/shard_map/pallas_call | solution.py:485
  13.9 0.8 %copy.7 = bf16[2048,128]{1,0:T(8,128)(2,1)} copy(bf16[2048,128]{1,0:T(8,128)(2,1)S(1)} %shard_map.55) | data formatting | bytes 1048576

commit v6 on v5

--- a/solution.py
+++ b/solution.py
@@ -350,7 +350,7 @@
             local[at, :] = tree_sum([weight_of[n] * held[n] for n in range(modes)])
             return held
 
-        lax.fori_loop(0, length, convolve, of_modes(start, 0), unroll=4)
+        lax.fori_loop(0, length, convolve, of_modes(start, 0), unroll=8)
 
     prefix_copy = pltpu.make_async_remote_copy(
         src_ref=prefix,
@@ -424,18 +424,7 @@
                 put_gated(at, skip_here, local[at, :] + tree_sum(held))
                 return held
 
-            if order == 0:
-                lax.fori_loop(0, length, finish, of_modes(carry, 0), unroll=4)
-                continue
-
-            def finish_some(row, held, finish=finish):
-                gated = gated_of(side, row)
-                for step in range(length // ROWS):
-                    held = finish(row * (length // ROWS) + step, held)
-                put_out(side, row, gated)
-                return held
-
-            lax.fori_loop(0, ROWS, finish_some, of_modes(carry, 0))
+            lax.fori_loop(0, length, finish, of_modes(carry, 0), unroll=8)
             for row in range(ROWS):
                 put_out(half, row, gated_of(half, row))
 

time: 14.9 us -> 14.4 us (0.966)
  Pallas kernels: 13.9 us -> 13.4 us
    pallas_call x1, Pallas kernels: 13.9 us -> 13.4 us  [body(): pl.pallas_call(call, out_shape=pltpu.VMEM((width, length), bf16), in_spec...]
where the time goes in v6:
time: 14.4 us; the launch traced here: 14.2 us
  Pallas kernels  13.4 us (93%)
  local copies, waits for them, and re-layouts  0.8 us (6%)
    pallas_call x1, Pallas kernels, body(): pl.pallas_call(call, out_shape=pltpu.VMEM((width, length), bf16), in_spec...  13.4 us
    unnamed x1, local copies, waits for them, and re-layouts  0.8 us

profile of v6, /device:TPU:5, one launch (start us, length us, event | category | flops | bytes accessed | tf_op | source)
XLA Modules:
  0.0 14.2 jit_solution(2081398258234483426)
XLA Ops:
  0.0 13.4 %shard_map.55 = bf16[2048,128]{1,0:T(8,128)(2,1)S(1)} custom-call(bf16[3,2048,128]{2,1,0:T(8,128)(2,1)} %projected.1, f32[3,3,8192]{2,1,0:T(4,128)} %taps_hbm.1, f32[64,128]{1,0:T(8,128)} %bitcast.3, f32[16,256]{1,0:T(8,128)} %bitcast.4, f32[16,256]{1,0:T(8,128)} %bitcast.5), custom_call_target="tpu_custom_call" | custom-call | tf_op jit(solution)/shard_map/pallas_call | solution.py:474
  13.4 0.8 %copy.7 = bf16[2048,128]{1,0:T(8,128)(2,1)} copy(bf16[2048,128]{1,0:T(8,128)(2,1)S(1)} %shard_map.55) | data formatting | bytes 1048576

commit v7 on v6

--- a/solution.py
+++ b/solution.py
@@ -135,11 +135,19 @@
         )
 
     def send_params(kind):
-        def send(step, _):
-            param_copy(kind, step).start()
-            return 0
-
-        lax.fori_loop(1, seq_count, send, 0)
+        first_side = 1 - lax.div(me, seq_count // 2)
+        for target_side in (first_side, 1 - first_side):
+
+            def send(ahead, _, target_side=target_side):
+                peer = 2 * lax.rem(pair + ahead, pair_count) + target_side
+
+                @pl.when(peer != me)
+                def _():
+                    param_copy(kind, lax.rem(peer - me + seq_count, seq_count)).start()
+
+                return 0
+
+            lax.fori_loop(0, pair_count, send, 0)
 
     send_params(0)
 
@@ -241,33 +249,36 @@
 
     mix_streams((1, 2), put_product)
 
-    def take_params(kind, target):
-        def take(step, _):
-            param_copy(kind, step).wait_recv()
+    def take_params(kind, target, half):
+        def take(sender, _):
+            @pl.when(sender != me)
+            def _():
+                param_copy(kind, lax.rem(me - sender + seq_count, seq_count)).wait_recv()
+
             return 0
 
-        lax.fori_loop(1, seq_count, take, 0)
-        for block in range(block_count):
-            half, row = divmod(block, ROWS)
+        first_sender = half * (seq_count // 2)
+        lax.fori_loop(first_sender, first_sender + seq_count // 2, take, 0)
+        for row in range(ROWS):
             if filters >= LANES:
                 per = filters // LANES
-                lane = (block % per) * LANES
-                piece = params[block // per, kind, :, lane : lane + LANES]
+                lane = (row % per) * LANES
+                piece = params[first_sender + row // per, kind, :, lane : lane + LANES]
             else:
                 per = LANES // filters
                 piece = jnp.concatenate(
-                    [params[block * per + part, kind] for part in range(per)], axis=1
+                    [params[first_sender + row * per + part, kind] for part in range(per)], axis=1
                 )
             target[pl.ds(half * mode_rows + row, modes, stride=ROWS), :] = piece
-
-    take_params(0, rates)
-    decay[...] = jnp.exp(-rates[...])
 
     def of_modes(ref, half):
         first = half * mode_rows
         return [ref[rows_of(first + n * ROWS), :] for n in range(modes)]
 
     def find_state(half):
+        here = rows_of(half * mode_rows, mode_rows)
+        take_params(0, rates, half)
+        decay[here, :] = jnp.exp(-rates[here, :])
         rate_of = of_modes(decay, half)
 
         def gather_state(t, held):
@@ -295,8 +306,6 @@
 
     find_state(1 - side)
     mate_copy(1 - side).start()
-    block_decay[...] = jnp.exp(-float(length) * rates[...])
-    pair_decay[...] = block_decay[...] * block_decay[...]
     find_state(side)
 
     @pl.when(side == 0)
@@ -320,6 +329,8 @@
 
         lax.fori_loop(pair + 1, pair_count, step, 0)
 
+    block_decay[...] = jnp.exp(-float(length) * rates[...])
+    pair_decay[...] = block_decay[...] * block_decay[...]
     mix_streams((0,), put_q)
     mate_copy(side).wait_recv()
     own_part = own_state[side].astype(jnp.float32)
@@ -329,7 +340,8 @@
     odd = jnp.where(side == 0, mate_part, own_part)
     pair_state[...] = (scale * even + odd).astype(jnp.bfloat16)
     for_later(lambda copy: copy.start())
-    take_params(1, weights)
+    for half in range(half_count):
+        take_params(1, weights, half)
 
     start[...] = jnp.zeros(start.shape, jnp.float32)
     for half in (1, 0):

time: 14.4 us -> 14.4 us (level)
  no operation moved by 1% of the time
where the time goes in v7:
time: 14.4 us; the launch traced here: 14.1 us
  Pallas kernels  13.3 us (92%)
  local copies, waits for them, and re-layouts  0.8 us (6%)
    pallas_call x1, Pallas kernels, body(): pl.pallas_call(call, out_shape=pltpu.VMEM((width, length), bf16), in_spec...  13.3 us
    unnamed x1, local copies, waits for them, and re-layouts  0.8 us

profile of v7, /device:TPU:5, one launch (start us, length us, event | category | flops | bytes accessed | tf_op | source)
XLA Modules:
  0.0 14.1 jit_solution(7596889484330630605)
XLA Ops:
  0.0 13.3 %shard_map.55 = bf16[2048,128]{1,0:T(8,128)(2,1)S(1)} custom-call(bf16[3,2048,128]{2,1,0:T(8,128)(2,1)} %projected.1, f32[3,3,8192]{2,1,0:T(4,128)} %taps_hbm.1, f32[64,128]{1,0:T(8,128)} %bitcast.3, f32[16,256]{1,0:T(8,128)} %bitcast.4, f32[16,256]{1,0:T(8,128)} %bitcast.5), custom_call_target="tpu_custom_call" | custom-call | tf_op jit(solution)/shard_map/pallas_call | solution.py:486
  13.3 0.8 %copy.7 = bf16[2048,128]{1,0:T(8,128)(2,1)} copy(bf16[2048,128]{1,0:T(8,128)(2,1)S(1)} %shard_map.55) | data formatting | bytes 1048576

commit v8 on v7

--- a/solution.py
+++ b/solution.py
@@ -225,7 +225,7 @@
                 return now, before
 
             first = [[laid_row(s, half, t) for s in which] for t in range(2)]
-            lax.fori_loop(2, length, mix, (first[1], first[0]), unroll=6)
+            lax.fori_loop(2, length, mix, (first[1], first[0]), unroll=14)
 
         for s in which:
             take_halo(s)
@@ -290,7 +290,7 @@
             length,
             gather_state,
             [jnp.zeros((ROWS, LANES), jnp.float32)] * modes,
-            unroll=8,
+            unroll=16,
         )
         own_state[half] = jnp.concatenate(held, axis=0).astype(jnp.bfloat16)
 
@@ -362,7 +362,7 @@
             local[at, :] = tree_sum([weight_of[n] * held[n] for n in range(modes)])
             return held
 
-        lax.fori_loop(0, length, convolve, of_modes(start, 0), unroll=8)
+        lax.fori_loop(0, length, convolve, of_modes(start, 0), unroll=16)
 
     prefix_copy = pltpu.make_async_remote_copy(
         src_ref=prefix,
@@ -408,7 +408,7 @@
                 put_gated(at, skip_here, local[at, :])
                 return 0
 
-            lax.fori_loop(0, length, finish, 0, unroll=8)
+            lax.fori_loop(0, length, finish, 0, unroll=16)
             for row in range(ROWS):
                 put_out(half, row, gated_of(half, row))
 
@@ -436,7 +436,7 @@
                 put_gated(at, skip_here, local[at, :] + tree_sum(held))
                 return held
 
-            lax.fori_loop(0, length, finish, of_modes(carry, 0), unroll=8)
+            lax.fori_loop(0, length, finish, of_modes(carry, 0), unroll=16)
             for row in range(ROWS):
                 put_out(half, row, gated_of(half, row))
 

time: 14.4 us -> 14.2 us (0.986)
  Pallas kernels: 13.3 us -> 13.1 us
    pallas_call x1, Pallas kernels: 13.3 us -> 13.1 us  [body(): pl.pallas_call(call, out_shape=pltpu.VMEM((width, length), bf16), in_spec...]
where the time goes in v8:
time: 14.2 us; the launch traced here: 13.9 us
  Pallas kernels  13.1 us (92%)
  local copies, waits for them, and re-layouts  0.8 us (6%)
    pallas_call x1, Pallas kernels, body(): pl.pallas_call(call, out_shape=pltpu.VMEM((width, length), bf16), in_spec...  13.1 us
    unnamed x1, local copies, waits for them, and re-layouts  0.8 us

profile of v8, /device:TPU:5, one launch (start us, length us, event | category | flops | bytes accessed | tf_op | source)
XLA Modules:
  0.0 13.9 jit_solution(5919926552014520777)
XLA Ops:
  0.0 13.1 %shard_map.55 = bf16[2048,128]{1,0:T(8,128)(2,1)S(1)} custom-call(bf16[3,2048,128]{2,1,0:T(8,128)(2,1)} %projected.1, f32[3,3,8192]{2,1,0:T(4,128)} %taps_hbm.1, f32[64,128]{1,0:T(8,128)} %bitcast.3, f32[16,256]{1,0:T(8,128)} %bitcast.4, f32[16,256]{1,0:T(8,128)} %bitcast.5), custom_call_target="tpu_custom_call" | custom-call | tf_op jit(solution)/shard_map/pallas_call | solution.py:486
  13.2 0.8 %copy.7 = bf16[2048,128]{1,0:T(8,128)(2,1)} copy(bf16[2048,128]{1,0:T(8,128)(2,1)S(1)} %shard_map.55) | data formatting | bytes 1048576

commit v9 on v8

--- a/solution.py
+++ b/solution.py
@@ -94,10 +94,11 @@
     residue_copy = pltpu.make_async_copy(residue_hbm, residue, tap_sem.at[3])
     rate_copy.start()
     residue_copy.start()
-    for s in (1, 2, 0):
-        in_copies[s].start()
+    in_copies[1].start()
     tap_copy.start()
+    in_copies[2].start()
     skip_copy.start()
+    in_copies[0].start()
 
     def turn(s):
         in_copies[s].wait()
@@ -121,6 +122,14 @@
     own_params[1] = residue[...] * jnp.sqrt(rate[...])
     params[me] = own_params[...]
     turn(1)
+    tap_copy.wait()
+    skip_copy.wait()
+    for lag in range(3):
+        for s in range(3):
+            for block in range(block_count):
+                taps[lag * 3 + s, block : block + 1, :] = taps_raw[
+                    lag, s : s + 1, block * LANES : (block + 1) * LANES
+                ]
     pl.semaphore_wait(barrier, seq_count - 1)
 
     def param_copy(kind, step):
@@ -189,15 +198,6 @@
     turn(0)
     send_halo(0)
     send_params(1)
-    tap_copy.wait()
-    skip_copy.wait()
-    for lag in range(3):
-        for s in range(3):
-            for block in range(block_count):
-                taps[lag * 3 + s, block : block + 1, :] = taps_raw[
-                    lag, s : s + 1, block * LANES : (block + 1) * LANES
-                ]
-
     def mix_streams(which, put):
         taps_of = [
             [

time: 14.2 us -> 14.2 us (level)
  no operation moved by 1% of the time
where the time goes in v9:
time: 14.2 us; the launch traced here: 14 us
  Pallas kernels  13.2 us (93%)
  local copies, waits for them, and re-layouts  0.8 us (6%)
    pallas_call x1, Pallas kernels, body(): pl.pallas_call(call, out_shape=pltpu.VMEM((width, length), bf16), in_spec...  13.2 us
    unnamed x1, local copies, waits for them, and re-layouts  0.8 us

profile of v9, /device:TPU:5, one launch (start us, length us, event | category | flops | bytes accessed | tf_op | source)
XLA Modules:
  0.0 14.0 jit_solution(12931735017384929222)
XLA Ops:
  0.0 13.2 %shard_map.55 = bf16[2048,128]{1,0:T(8,128)(2,1)S(1)} custom-call(bf16[3,2048,128]{2,1,0:T(8,128)(2,1)} %projected.1, f32[3,3,8192]{2,1,0:T(4,128)} %taps_hbm.1, f32[64,128]{1,0:T(8,128)} %bitcast.3, f32[16,256]{1,0:T(8,128)} %bitcast.4, f32[16,256]{1,0:T(8,128)} %bitcast.5), custom_call_target="tpu_custom_call" | custom-call | tf_op jit(solution)/shard_map/pallas_call | solution.py:486
  13.2 0.8 %copy.7 = bf16[2048,128]{1,0:T(8,128)(2,1)} copy(bf16[2048,128]{1,0:T(8,128)(2,1)S(1)} %shard_map.55) | data formatting | bytes 1048576
